TPU v7x, 128 devices: a whole 4x4x4 slice. The times are simulated.
128 devices in a mesh: ang: 8 (over z, x_hi), pos: 16 (over y, x_lo, core).
Axes of the slice: x: 4 (x_hi: 2, x_lo: 2; x = x_hi * 2 + x_lo), y: 4, z: 4, core: 2. Of those that a mesh axis runs over, the one named last changes fastest.
Arguments:
- object_init: float32 [16, 2, 512, 512], P('ang', None, 'pos'), may hold values from -4 to 4
- probe_field: float32 [2, 512, 512], replicated, may hold values from -4 to 4
- amplitudes: float32 [16, 16, 512, 512], P('ang', 'pos'), may hold values from 0.2 to 2
- offsets: int32 [16, 16, 2], P('ang', 'pos'), may hold values from 0 to 511
- slot_angle: int32 [16], replicated, may hold values from 0 to 15, each once
- conv_first: bfloat16 [3, 3, 32, 2], replicated, may hold values from -2 to 2
- bias_first: float32 [32], replicated, may hold values from -3 to 3
- conv_middle: bfloat16 [2, 3, 3, 32, 32], replicated, may hold values from -0.5 to 0.5
- bias_middle: float32 [2, 32], replicated, may hold values from -3 to 3
- conv_last: bfloat16 [3, 3, 32], replicated, may hold values from -0.5 to 0.5
Outputs:
- object_final: float32 [16, 2, 512, 512], P('ang', None, 'pos')
- projections: float32 [16, 8, 4, 16, 512], P('pos', 'ang')
Inputs may be any that keep to these rules, and one draw needn't show every extreme that they name: `slot_angle`: each of the 16 angles is held by exactly one slot.
All inputs are finite; a program needn't handle non-finite values.
Results may differ from a plain program's by a relative error of at most 0.035.
Values may be sent and summed in bfloat16 or wider, within the bound.
A program may use at most 128 MiB of HBM per device.

v0:
```python
import functools

import jax
import jax.numpy as jnp
import ml_dtypes
import numpy as np
from jax import lax
from jax.experimental import pallas as pl
from jax.experimental.pallas import tpu as pltpu
from jax.sharding import PartitionSpec as P

soften = 0.25
learning = 1.5
N = 512
B = 128
f32 = jnp.float32
bf16 = jnp.bfloat16
MESH = pl.DeviceIdType.MESH


def make_tables():
    f = np.arange(N)
    g = np.where(f < N // 2, f, f - N).astype(np.float64)
    lam = np.exp(-3j * np.pi * g * g / (4 * N))
    d = np.arange(B)[:, None] - np.arange(B)[None, :]
    blocks = []
    for m in range(4):
        fm = np.arange(m, N, 4)
        c = (lam[fm] * np.exp(2j * np.pi * fm * d[:, :, None] / N)).sum(-1) / N
        blocks.append(np.block([[c.real, -c.imag], [c.imag, c.real]]))
    left = np.stack(blocks)
    turned = np.ascontiguousarray(np.swapaxes(left, 1, 2))
    return left.astype(ml_dtypes.bfloat16), turned.astype(ml_dtypes.bfloat16)


def add(a, b):
    return (a[0] + b[0], a[1] + b[1])


def sub(a, b):
    return (a[0] - b[0], a[1] - b[1])


def add_i(a, b):
    return (a[0] - b[1], a[1] + b[0])


def sub_i(a, b):
    return (a[0] + b[1], a[1] - b[0])


def fold(x):
    t0, t1, t2, t3 = add(x[0], x[2]), sub(x[0], x[2]), add(x[1], x[3]), sub(x[1], x[3])
    return [add(t0, t2), sub_i(t1, t3), sub(t0, t2), add_i(t1, t3)]


def unfold(x):
    t0, t1, t2, t3 = add(x[0], x[2]), sub(x[0], x[2]), add(x[1], x[3]), sub(x[1], x[3])
    return [add(t0, t2), add_i(t1, t3), sub(t0, t2), sub_i(t1, t3)]


def fold2(e):
    rows = [fold(e[q]) for q in range(4)]
    cols = [fold([rows[q][m] for q in range(4)]) for m in range(4)]
    return [[cols[mc][mr] for mc in range(4)] for mr in range(4)]


def unfold2(e):
    cols = [unfold([e[q][m] for q in range(4)]) for m in range(4)]
    return [unfold([cols[m][q] for m in range(4)]) for q in range(4)]


def lanes(q):
    return slice(q * B, q * B + B)


def store_y(ya, y, row, n):
    for mr in range(4):
        for mc in range(4):
            for ri in range(2):
                ya[pl.ds((mr * 2 + ri) * B + row, n), lanes(mc)] = y[mr][mc][ri].astype(bf16)


def load_f(f, row, n):
    return [
        [
            tuple(f[pl.ds((mr * 2 + ri) * B + row, n), lanes(mc)] for ri in range(2))
            for mc in range(4)
        ]
        for mr in range(4)
    ]


ROWS = 16


def stage1(v, pr, ya):
    n = ROWS

    def body(g, _):
        row = pl.multiple_of(g * n, n)
        tile = g * n // 32
        part = pl.multiple_of(lax.rem(g * n, 32), n)
        e = []
        for q in range(4):
            line = []
            for c in range(4):
                vr = v[q * 4 + tile, 0, pl.ds(part, n), lanes(c)].astype(f32)
                vi = v[q * 4 + tile, 1, pl.ds(part, n), lanes(c)].astype(f32)
                a = pr[0, pl.ds(q * B + row, n), lanes(c)].astype(f32)
                b = pr[1, pl.ds(q * B + row, n), lanes(c)].astype(f32)
                line.append((a * vr - b * vi, a * vi + b * vr))
            e.append(line)
        store_y(ya, fold2(e), row, n)
        return 0

    lax.fori_loop(0, B // n, body, 0)


def right(ya, mats, out, dtype):
    for mc in range(4):
        lhs = jnp.concatenate(
            [
                jnp.concatenate(
                    [
                        ya[(mr * 2 + ri) * B : (mr * 2 + ri + 1) * B, lanes(mc)]
                        for ri in range(2)
                    ],
                    1,
                )
                for mr in range(4)
            ],
            0,
        )
        r = jnp.dot(lhs, mats[mc], preferred_element_type=f32)
        for mr in range(4):
            for ri in range(2):
                out[(mr * 2 + ri) * B : (mr * 2 + ri + 1) * B, lanes(mc)] = r[
                    mr * B : mr * B + B, lanes(ri)
                ].astype(dtype)


def left(mats, yb, out, dtype):
    for mr in range(4):
        out[mr * 256 : mr * 256 + 256, :] = jnp.dot(
            mats[mr], yb[mr * 256 : mr * 256 + 256, :], preferred_element_type=f32
        ).astype(dtype)


def stage2(f, am, ya):
    n = ROWS

    def body(g, _):
        row = pl.multiple_of(g * n, n)
        w = unfold2(load_f(f, row, n))
        for q in range(4):
            for c in range(4):
                wr, wi = w[q][c]
                a = am[pl.ds(q * B + row, n), lanes(c)].astype(f32)
                s = 1.0 - a * lax.rsqrt(wr * wr + wi * wi + soften)
                w[q][c] = (wr * s, wi * s)
        store_y(ya, fold2(w), row, n)
        return 0

    lax.fori_loop(0, B // n, body, 0)


def stage3(f, pr, g, x, cls):
    n = ROWS

    def body(k, _):
        part = pl.multiple_of(k * n, n)
        row = pl.multiple_of((2 * x + cls) * 32 + k * n, n)
        tot = None
        for i in range(2):
            w = unfold2(load_f(f.at[i], row, n))
            new = []
            for q in range(4):
                for c in range(4):
                    a = pr[i, 0, pl.ds(q * B + row, n), lanes(c)].astype(f32)
                    b = pr[i, 1, pl.ds(q * B + row, n), lanes(c)].astype(f32)
                    br, bi = w[q][c]
                    new.append((a * br + b * bi, a * bi - b * br))
            tot = new if tot is None else [add(p, q) for p, q in zip(tot, new)]
        for q in range(4):
            for c in range(4):
                for ri in range(2):
                    g[q, ri, pl.ds(part, n), lanes(c)] = tot[q * 4 + c][ri].astype(g.dtype)
        return 0

    lax.fori_loop(0, 32 // n, body, 0)


def one_hot(offset, transpose):
    a = lax.broadcasted_iota(jnp.int32, (N, N), 0)
    b = lax.broadcasted_iota(jnp.int32, (N, N), 1)
    if transpose:
        return jnp.where(a == ((b + offset) & (N - 1)), 1.0, 0.0).astype(bf16)
    return jnp.where(b == ((a + offset) & (N - 1)), 1.0, 0.0).astype(bf16)


def make_hot(off, hot):
    hot[0] = one_hot(off[0:1, 0:1], False)
    hot[1] = one_hot(off[8:9, 0:1], True)


def roll_plane(src, hot, tmp, dst):
    for h in range(2):
        sl = slice(h * 256, h * 256 + 256)
        tmp[sl, :] = jnp.dot(hot[0, sl, :], src[...], preferred_element_type=f32).astype(bf16)
    for h in range(2):
        sl = slice(h * 256, h * 256 + 256)
        dst[sl, :] = jnp.dot(tmp[sl, :], hot[1], preferred_element_type=f32).astype(bf16)


def main_kernel(
    obj,
    probe_hbm,
    amps_hbm,
    off,
    mat_l,
    mat_r,
    obj_out,
    nb_out,
    view,
    probe_in,
    amps_in,
    probe16,
    amp16,
    amp_send,
    amp_recv,
    off_own,
    off_send,
    off_recv,
    hot,
    tmp,
    pr,
    am,
    ya,
    yb,
    ff,
    x_obj,
    g_send,
    g_recv,
    g_own,
    sa,
    sb,
    ra,
    rb,
    total,
    xg_send,
    xg_recv,
    as_send,
    nb,
    local_sem,
    x_sem,
    ag_recv,
    ring_send,
    sib_send,
    gs_sem,
    gr_sem,
    sa_sem,
    sb_sem,
    ra_sem,
    rb_sem,
    aa_send,
    aa_recv,
):
    pos = lax.axis_index("pos")
    ang = lax.axis_index("ang")
    c = lax.rem(pos, 2)
    s = lax.rem(pos // 2, 2)
    y = pos // 4
    up = lax.rem(y + 1, 4)
    down = lax.rem(y + 3, 4)
    far = lax.rem(y + 2, 4)

    def at(yy, xx, cc):
        return yy * 4 + xx * 2 + cc

    dev_up = (ang, at(up, s, c))
    dev_down = (ang, at(down, s, c))
    dev_x = (ang, at(y, 1 - s, c))
    dev_sib = (ang, at(y, s, 1 - c))
    step_size = learning / 16

    def rc(src, dst, send, recv, dev):
        return pltpu.make_async_remote_copy(
            src_ref=src, dst_ref=dst, send_sem=send, recv_sem=recv, device_id=dev,
            device_id_type=MESH,
        )

    def arrived(dst, recv):
        rc(dst, dst, recv, recv, dev_x).wait_recv()

    def left_dev(src, send):
        rc(src, src, send, send, dev_x).wait_send()

    cp_probe = pltpu.make_async_copy(probe_hbm, probe_in, local_sem.at[0])
    cp_amps = pltpu.make_async_copy(amps_hbm, amps_in, local_sem.at[1])
    cp_amps.start()
    cp_probe.start()

    barrier = pltpu.get_barrier_semaphore()
    for dev in (dev_up, dev_down, dev_x, dev_sib):
        pl.semaphore_signal(barrier, inc=1, device_id=dev, device_id_type=MESH)
    for d in range(1, 8):
        pl.semaphore_signal(
            barrier, inc=1, device_id=(lax.rem(ang + d, 8), pos), device_id_type=MESH
        )

    own = at(y, s, c)
    other = at(y, 1 - s, c)
    view[0, own] = obj[s].astype(bf16)
    x_obj[...] = obj[1 - s].astype(bf16)
    for i, (ref, slot) in enumerate(((off_own, s), (off_send, 1 - s))):
        for k in range(2):
            value = jnp.where(slot == 0, off[0, 0, k], off[1, 0, k])
            ref[k * 8 : k * 8 + 8, :] = jnp.full((8, 128), value, jnp.int32)

    pl.semaphore_wait(barrier, 11)

    rc(x_obj, view.at[0, own], x_sem.at[0], ag_recv.at[0, own], dev_x).start()
    rc(off_send, off_recv, x_sem.at[1], x_sem.at[2], dev_x).start()

    def ag_start(k, xx):
        tile = at(y, xx, c)
        ref = view.at[k, tile]
        rc(ref, ref, ring_send.at[k, xx, 0], ag_recv.at[k, tile], dev_up).start()
        rc(ref, ref, ring_send.at[k, xx, 1], ag_recv.at[k, tile], dev_down).start()
        rc(ref, ref, sib_send.at[k, 0, xx], ag_recv.at[k, tile], dev_sib).start()

    def ag_take(k, yy, xx, rel, forward):
        tile = at(yy, xx, c)
        ref = view.at[k, tile]
        arrived(ref, ag_recv.at[k, tile])
        if forward is not None:
            rc(ref, ref, ring_send.at[k, 2, forward], ag_recv.at[k, tile],
               dev_up if forward == 0 else dev_down).start()
        rc(ref, ref, sib_send.at[k, rel, xx], ag_recv.at[k, tile], dev_sib).start()

    def ag_relay(k):
        ag_take(k, down, 0, 1, 0)
        ag_take(k, up, 1, 2, 1)

    def ag_finish(k):
        ag_take(k, down, 1, 1, None)
        ag_take(k, up, 0, 2, None)
        ag_take(k, far, 0, 3, None)
        ag_take(k, far, 1, 3, None)
        for yy in range(4):
            for xx in range(2):
                tile = at(yy, xx, 1 - c)
                arrived(view.at[k, tile], ag_recv.at[k, tile])

    def ag_sent(k):
        for xx in range(2):
            tile = at(y, xx, c)
            for d in range(2):
                left_dev(view.at[k, tile], ring_send.at[k, xx, d])
        left_dev(view.at[k, at(down, 0, c)], ring_send.at[k, 2, 0])
        left_dev(view.at[k, at(up, 1, c)], ring_send.at[k, 2, 1])
        for rel, yy in enumerate((y, down, up, far)):
            for xx in range(2):
                left_dev(view.at[k, at(yy, xx, c)], sib_send.at[k, rel, xx])

    ag_start(0, s)
    cp_amps.wait()
    amp_send[...] = amps_in[1 - s, 0].astype(bf16)
    cp_amp_x = rc(amp_send, amp_recv, x_sem.at[3], x_sem.at[4], dev_x)
    cp_amp_x.start()
    amp16[...] = amps_in[s, 0].astype(bf16)
    arrived(view.at[0, other], ag_recv.at[0, other])
    ag_start(0, 1 - s)
    cp_probe.wait()
    probe16[...] = probe_in[...].astype(bf16)
    make_hot(off_own, hot.at[0])
    roll_plane(probe16.at[0], hot.at[0], tmp, pr.at[0, 0])
    roll_plane(probe16.at[1], hot.at[0], tmp, pr.at[0, 1])
    ag_relay(0)
    roll_plane(amp16, hot.at[0], tmp, am.at[0])
    arrived(off_recv, x_sem.at[2])
    make_hot(off_recv, hot.at[1])
    roll_plane(probe16.at[0], hot.at[1], tmp, pr.at[1, 0])
    roll_plane(probe16.at[1], hot.at[1], tmp, pr.at[1, 1])

    for k in range(2):
        if k == 1:
            ag_relay(k)
        ag_finish(k)
        for i in range(2):
            stage1(view.at[k], pr.at[i], ya.at[i])
            right(ya.at[i], mat_r, yb.at[i], bf16)
            left(mat_l, yb.at[i], ff.at[i], f32)
        if k == 0:
            arrived(amp_recv, x_sem.at[4])
            roll_plane(amp_recv, hot.at[1], tmp, am.at[1])
        for i in range(2):
            stage2(ff.at[i], am.at[i], ya.at[i])
            left(mat_r, ya.at[i], yb.at[i], bf16)
            right(yb.at[i], mat_l, ff.at[i], f32)
        for xx in range(2):
            stage3(ff, pr, g_send.at[k, xx], xx, 1 - c)
            rc(g_send.at[k, xx], g_recv.at[k, xx], gs_sem.at[k, xx], gr_sem.at[k, xx],
               dev_sib).start()
        for xx in range(2):
            stage3(ff, pr, g_own.at[xx], xx, c)
        ag_sent(k)

        def comb(yy, xx):
            return g_own[xx, yy] + g_recv[k, xx, yy].astype(f32)

        def push(buf, sem, dst, dsem, j, value, dev):
            buf[k, j] = value.astype(bf16)
            rc(buf.at[k, j], dst.at[k, j], sem.at[k, j], dsem.at[k, j], dev).start()

        arrived(g_recv.at[k, 0], gr_sem.at[k, 0])
        push(sa, sa_sem, ra, ra_sem, 0, comb(far, 0), dev_up)
        arrived(g_recv.at[k, 1], gr_sem.at[k, 1])
        push(sb, sb_sem, rb, rb_sem, 0, comb(far, 1), dev_down)
        push(sa, sa_sem, ra, ra_sem, 2, comb(up, 1), dev_up)
        push(sb, sb_sem, rb, rb_sem, 2, comb(down, 0), dev_down)
        arrived(ra.at[k, 0], ra_sem.at[k, 0])
        push(sa, sa_sem, ra, ra_sem, 1, comb(up, 0) + ra[k, 0].astype(f32), dev_up)
        arrived(rb.at[k, 0], rb_sem.at[k, 0])
        push(sb, sb_sem, rb, rb_sem, 1, comb(down, 1) + rb[k, 0].astype(f32), dev_down)
        for j in (2, 1):
            arrived(ra.at[k, j], ra_sem.at[k, j])
            arrived(rb.at[k, j], rb_sem.at[k, j])
        t0 = comb(y, 0) + ra[k, 1].astype(f32) + rb[k, 2].astype(f32)
        t1 = comb(y, 1) + ra[k, 2].astype(f32) + rb[k, 1].astype(f32)
        if k == 0:
            total[0] = t0
            total[1] = t1
            view[1, own] = (obj[s] - step_size * total[s]).astype(bf16)
            view[1, other] = (
                view[0, other].astype(f32) - step_size * total[1 - s]
            ).astype(bf16)
            ag_start(1, 0)
            ag_start(1, 1)
        else:
            total[0] = total[0] + t0
            total[1] = total[1] + t1
        for j in range(3):
            left_dev(sa.at[k, j], sa_sem.at[k, j])
            left_dev(sb.at[k, j], sb_sem.at[k, j])
        for xx in range(2):
            left_dev(g_send.at[k, xx], gs_sem.at[k, xx])

    xg_send[...] = total[1 - s].astype(bf16)
    cp_xg = rc(xg_send, xg_recv, x_sem.at[5], x_sem.at[6], dev_x)
    cp_xg.start()
    obj_out[s] = obj[s] - step_size * total[s]
    cp_xg.wait_recv()
    obj_out[1 - s] = obj[1 - s] - step_size * xg_recv[...].astype(f32)
    for g in range(8):
        as_send[g] = jnp.concatenate(
            [obj_out[sl, ri, g * 4 : g * 4 + 4, :] for sl in range(2) for ri in range(2)], 0
        ).astype(bf16)

    def a2a(d):
        to = lax.rem(ang + d, 8)
        return rc(as_send.at[to], nb.at[ang], aa_send.at[d], aa_recv.at[ang], (to, pos))

    for d in range(1, 8):
        a2a(d).start()
    nb[ang] = as_send[ang]
    for d in range(1, 8):
        frm = lax.rem(ang + d, 8)
        arrived(nb.at[frm], aa_recv.at[frm])
    nb_out[...] = nb[...]
    for d in range(1, 8):
        a2a(d).wait_send()
    cp_xg.wait_send()
    left_dev(x_obj, x_sem.at[0])
    left_dev(off_send, x_sem.at[1])
    cp_amp_x.wait_send()


def sweeps(object_init, probe_field, amplitudes, offsets):
    mat_l, mat_r = make_tables()
    vm = pl.BlockSpec(memory_space=pltpu.VMEM)
    hbm = pl.BlockSpec(memory_space=pl.ANY)
    tile = (2, 32, N)
    scratch = [
        pltpu.VMEM((2, 16) + tile, bf16),
        pltpu.VMEM((2, N, N), f32),
        pltpu.VMEM((2, 1, N, N), f32),
        pltpu.VMEM((2, N, N), bf16),
        pltpu.VMEM((N, N), bf16),
        pltpu.VMEM((N, N), bf16),
        pltpu.VMEM((N, N), bf16),
        pltpu.VMEM((16, 128), jnp.int32),
        pltpu.VMEM((16, 128), jnp.int32),
        pltpu.VMEM((16, 128), jnp.int32),
        pltpu.VMEM((2, 2, N, N), bf16),
        pltpu.VMEM((N, N), bf16),
        pltpu.VMEM((2, 2, N, N), bf16),
        pltpu.VMEM((2, N, N), bf16),
        pltpu.VMEM((2, 2 * N, N), bf16),
        pltpu.VMEM((2, 2 * N, N), bf16),
        pltpu.VMEM((2, 2 * N, N), f32),
        pltpu.VMEM(tile, bf16),
        pltpu.VMEM((2, 2, 4) + tile, bf16),
        pltpu.VMEM((2, 2, 4) + tile, bf16),
        pltpu.VMEM((2, 4) + tile, f32),
        pltpu.VMEM((2, 3) + tile, bf16),
        pltpu.VMEM((2, 3) + tile, bf16),
        pltpu.VMEM((2, 3) + tile, bf16),
        pltpu.VMEM((2, 3) + tile, bf16),
        pltpu.VMEM((2,) + tile, f32),
        pltpu.VMEM(tile, bf16),
        pltpu.VMEM(tile, bf16),
        pltpu.VMEM((8, 16, N), bf16),
        pltpu.VMEM((8, 16, N), bf16),
        pltpu.SemaphoreType.DMA((2,)),
        pltpu.SemaphoreType.DMA((7,)),
        pltpu.SemaphoreType.DMA((2, 16)),
        pltpu.SemaphoreType.DMA((2, 3, 2)),
        pltpu.SemaphoreType.DMA((2, 4, 2)),
        pltpu.SemaphoreType.DMA((2, 2)),
        pltpu.SemaphoreType.DMA((2, 2)),
        pltpu.SemaphoreType.DMA((2, 3)),
        pltpu.SemaphoreType.DMA((2, 3)),
        pltpu.SemaphoreType.DMA((2, 3)),
        pltpu.SemaphoreType.DMA((2, 3)),
        pltpu.SemaphoreType.DMA((8,)),
        pltpu.SemaphoreType.DMA((8,)),
    ]
    return pl.pallas_call(
        main_kernel,
        out_shape=(
            jax.ShapeDtypeStruct((2,) + tile, f32),
            jax.ShapeDtypeStruct((8, 16, N), bf16),
        ),
        in_specs=[vm, hbm, hbm, pl.BlockSpec(memory_space=pltpu.SMEM), vm, vm],
        out_specs=(vm, vm),
        scratch_shapes=scratch,
        compiler_params=pltpu.CompilerParams(
            collective_id=0, has_side_effects=True, vmem_limit_bytes=48 << 20
        ),
        cost_estimate=pl.CostEstimate(
            flops=12_000_000_000, bytes_accessed=8_000_000, transcendentals=1_000_000
        ),
    )(object_init, probe_field, amplitudes, offsets, jnp.asarray(mat_l), jnp.asarray(mat_r))


def shift_along(values, offset, axis):
    if offset == 0:
        return values
    length = values.shape[axis]
    padding = jnp.zeros_like(lax.slice_in_dim(values, 0, 1, axis=axis))
    if offset > 0:
        return jnp.concatenate([lax.slice_in_dim(values, 1, length, axis=axis), padding], axis)
    return jnp.concatenate([padding, lax.slice_in_dim(values, 0, length - 1, axis=axis)], axis)


def conv_layer(inputs, weights):
    running = None
    for row_tap in range(3):
        along_angle = shift_along(inputs, row_tap - 1, 2)
        stacked = jnp.concatenate(
            [shift_along(along_angle, col_tap - 1, 3) for col_tap in range(3)], 0
        )
        merged = jnp.concatenate([weights[row_tap, col_tap] for col_tap in range(3)], 1)
        piece_sum = jnp.einsum("oc,csaw->osaw", merged, stacked, preferred_element_type=jnp.float32)
        running = piece_sum if running is None else running + piece_sum
    return running


def network(inputs, conv_first, bias_first, conv_middle, bias_middle, conv_last):
    hidden = jax.nn.relu(conv_layer(inputs, conv_first) + bias_first[:, None, None, None]).astype(
        jnp.bfloat16
    )
    for layer_index in range(conv_middle.shape[0]):
        raised = (
            conv_layer(hidden, conv_middle[layer_index])
            + bias_middle[layer_index][:, None, None, None]
        )
        hidden = jax.nn.relu(raised).astype(jnp.bfloat16)
    return conv_layer(hidden, conv_last[:, :, None, :])[0]


def reorder_angles(height_slabs, slot_angle):
    count = height_slabs.shape[0]
    selector = (slot_angle[None, :] == jnp.arange(count, dtype=jnp.int32)[:, None]).astype(
        jnp.bfloat16
    )
    return jnp.einsum(
        "kj,jcsw->cskw", selector, height_slabs, preferred_element_type=jnp.float32
    ).astype(jnp.bfloat16)


def on_device(
    object_init,
    probe_field,
    amplitudes,
    offsets,
    slot_angle,
    conv_first,
    bias_first,
    conv_middle,
    bias_middle,
    conv_last,
):
    object_tile, slabs = sweeps(object_init, probe_field, amplitudes, offsets)
    ordered = reorder_angles(slabs.reshape(16, 2, 4, N), slot_angle)
    outputs = network(ordered, conv_first, bias_first, conv_middle, bias_middle, conv_last)
    return (object_tile, outputs[None, None])


def solution(mesh):
    return jax.shard_map(
        on_device,
        mesh=mesh,
        in_specs=(
            P("ang", None, "pos", None),
            P(),
            P("ang", "pos", None, None),
            P("ang", "pos", None),
            P(),
            P(),
            P(),
            P(),
            P(),
            P(),
        ),
        out_specs=(P("ang", None, "pos", None), P("pos", "ang", None, None, None)),
        check_vma=False,
    )
```

profile of v0, /device:TPU:0, one launch (start us, length us, event | category | flops | bytes accessed | tf_op | source)
XLA Modules:
  0.0 113.2 jit_solution(16239466238011364196)
XLA Ops:
  0.6 1.6 %copy-done = f32[2,512,512]{2,1,0:T(8,128)S(1)} copy-done((f32[2,512,512]{2,1,0:T(8,128)S(1)}, f32[2,512,512]{2,1,0:T(8,128)}, u32[]{:S(2)}) %copy-start) | copy-done | bytes 2097176
  2.2 1.6 %copy-done.1 = f32[2,1,512,512]{3,2,1,0:T(8,128)S(1)} copy-done((f32[2,1,512,512]{3,2,1,0:T(8,128)S(1)}, f32[2,1,512,512]{3,2,1,0:T(8,128)}, u32[]{:S(2)}) %copy-start.1) | copy-done | bytes 2097176
  3.8 0.9 copy-done.2
  4.8 0.7 copy-done.3
  5.4 1.0 copy-done.4
  6.5 1.0 copy-done.5
  7.5 72.6 %shard_map.131 = (f32[2,2,32,512]{3,2,1,0:T(8,128)S(1)}, bf16[8,16,512]{2,1,0:T(8,128)(2,1)S(1)}) custom-call(f32[2,2,32,512]{3,2,1,0:T(8,128)S(1)} %copy-done.2, f32[2,512,512]{2,1,0:T(8,128)S(1)} %copy-done, f32[2,1,512,512]{3,2,1,0:T(8,128)S(1)} %copy-done.1, s32[2,1,2]{2,1,0:T(1,128)S(1)} %copy-done.3, bf16[4,256,256]{2,1,0:T(8,128)(2,1)S(1)} %copy-done.4, ...), custom_call_target="tpu_custom_call" | custom-call | flops 12000000000 | bytes 8000000 | tf_op jit(solution)/shard_map/pallas_call | solution.py:530
  80.2 0.2 fusion.103
  80.4 0.2 pad_slice_fusion.1
  80.6 0.1 fusion.116
  80.7 0.8 fusion.113
  81.5 0.0 copy-start.11
  81.5 0.1 fusion.220
  81.6 0.1 fusion.118
  81.7 0.8 fusion.111
  82.5 0.1 fusion.120
  82.7 1.4 %maximum_convert_fusion.2 = bf16[32,4,16,512]{3,0,2,1:T(8,128)(2,1)S(1)} fusion(f32[32,4,16,512]{3,0,2,1:T(8,128)S(1)} %fusion.113, f32[32,4,16,512]{3,0,2,1:T(8,128)S(1)} %fusion.111, f32[32]{0:T(128)S(1)} %copy-done.11, bf16[6,4,16,512]{3,2,1,0:T(8,128)(2,1)S(1)} %fusion.120, bf16[32,2]{0,1:T(2,128)(2,1)S(1)} %get-tuple-element.65, ...), kind=kOutput, calls=%fused_computation.79 | convolution fusion | flops 17826944 | bytes 10879488 | tf_op jit(solution)/shard_map/oc,csaw->osaw/dot_general | solution.py:566
  84.0 0.5 fusion.217
  84.6 1.3 %pad_slice_fusion.15 = (bf16[32,4,16,511]{3,0,2,1:T(8,128)(2,1)S(1)}, bf16[32,4,16,511]{3,0,2,1:T(8,128)(2,1)S(1)}) fusion(bf16[32,4,15,512]{3,0,2,1:T(8,128)(2,1)S(1)} %get-tuple-element.15), kind=kLoop, calls=%fused_computation.271 | loop fusion | bytes 6152192 | tf_op jit(solution)/shard_map/slice | solution.py:555
  85.9 0.3 concatenate.185
  86.2 1.0 fusion.19
  87.3 1.4 %fusion.218 = (bf16[32,4,16,511]{3,0,2,1:T(8,128)(2,1)S(1)}, bf16[32,4,16,511]{3,0,2,1:T(8,128)(2,1)S(1)}) fusion(bf16[32,4,16,512]{3,0,2,1:T(8,128)(2,1)S(1)} %maximum_convert_fusion.2), kind=kLoop, calls=%fused_computation.277 | loop fusion | bytes 8372224 | tf_op jit(solution)/shard_map/slice | solution.py:555
  88.7 0.0 copy-start.9
  88.7 1.0 fusion.22
  89.7 1.2 %pad_slice_fusion.13 = (bf16[32,4,16,511]{3,0,2,1:T(8,128)(2,1)S(1)}, bf16[32,4,16,511]{3,0,2,1:T(8,128)(2,1)S(1)}) fusion(bf16[32,4,15,512]{3,0,2,1:T(8,128)(2,1)S(1)} %get-tuple-element.14), kind=kLoop, calls=%fused_computation.269 | loop fusion | bytes 6152192 | tf_op jit(solution)/shard_map/slice | solution.py:555
  91.0 0.2 concatenate.194
  91.2 2.0 %maximum_convert_fusion.1 = bf16[32,4,16,512]{3,0,2,1:T(8,128)(2,1)S(1)} fusion(f32[32,4,16,512]{3,0,2,1:T(8,128)S(1)} %fusion.19, f32[32,4,16,512]{3,0,2,1:T(8,128)S(1)} %fusion.22, f32[32]{0:T(128)S(1)} %get-tuple-element.77, bf16[32,4,16,511]{3,0,2,1:T(8,128)(2,1)S(1)} %get-tuple-element.27, bf16[32,4,16,511]{3,0,2,1:T(8,128)(2,1)S(1)} %get-tuple-element.26, ...), kind=kOutput, calls=%fused_computation.78 | convolution fusion | flops 238045184 | bytes 16775296 | tf_op jit(solution)/shard_map/oc,csaw->osaw/dot_general | solution.py:566
  93.2 0.5 fusion.215
  93.7 1.3 %pad_slice_fusion.11 = (bf16[32,4,16,511]{3,0,2,1:T(8,128)(2,1)S(1)}, bf16[32,4,16,511]{3,0,2,1:T(8,128)(2,1)S(1)}) fusion(bf16[32,4,15,512]{3,0,2,1:T(8,128)(2,1)S(1)} %get-tuple-element.11), kind=kLoop, calls=%fused_computation.267 | loop fusion | bytes 6152192 | tf_op jit(solution)/shard_map/slice | solution.py:555
  95.1 0.2 concatenate.198
  95.3 1.1 fusion.28
  96.3 1.3 %fusion.216 = (bf16[32,4,16,511]{3,0,2,1:T(8,128)(2,1)S(1)}, bf16[32,4,16,511]{3,0,2,1:T(8,128)(2,1)S(1)}) fusion(bf16[32,4,16,512]{3,0,2,1:T(8,128)(2,1)S(1)} %maximum_convert_fusion.1), kind=kLoop, calls=%fused_computation.275 | loop fusion | bytes 8372224 | tf_op jit(solution)/shard_map/slice | solution.py:555
  97.6 1.1 fusion.31
  98.7 1.2 %pad_slice_fusion.9 = (bf16[32,4,16,511]{3,0,2,1:T(8,128)(2,1)S(1)}, bf16[32,4,16,511]{3,0,2,1:T(8,128)(2,1)S(1)}) fusion(bf16[32,4,15,512]{3,0,2,1:T(8,128)(2,1)S(1)} %get-tuple-element.10), kind=kLoop, calls=%fused_computation.265 | loop fusion | bytes 6152192 | tf_op jit(solution)/shard_map/slice | solution.py:555
  100.0 0.2 concatenate.207
  100.2 1.9 %maximum_convert_fusion = bf16[32,4,16,512]{3,0,2,1:T(8,128)(2,1)S(1)} fusion(f32[32,4,16,512]{3,0,2,1:T(8,128)S(1)} %fusion.28, f32[32,4,16,512]{3,0,2,1:T(8,128)S(1)} %fusion.31, f32[32]{0:T(128)S(1)} %get-tuple-element.76, bf16[32,4,16,511]{3,0,2,1:T(8,128)(2,1)S(1)} %get-tuple-element.23, bf16[32,4,16,511]{3,0,2,1:T(8,128)(2,1)S(1)} %get-tuple-element.22, ...), kind=kOutput, calls=%fused_computation.77 | convolution fusion | flops 238045184 | bytes 16775296 | tf_op jit(solution)/shard_map/oc,csaw->osaw/dot_general | solution.py:566
  102.1 0.5 fusion.213
  102.6 0.0 copy-start.7
  102.6 1.3 %pad_slice_fusion.5 = (bf16[32,4,16,511]{3,0,2,1:T(8,128)(2,1)S(1)}, bf16[32,4,16,511]{3,0,2,1:T(8,128)(2,1)S(1)}) fusion(bf16[32,4,15,512]{3,0,2,1:T(8,128)(2,1)S(1)} %get-tuple-element.7), kind=kLoop, calls=%fused_computation.261 | loop fusion | bytes 6152192 | tf_op jit(solution)/shard_map/slice | solution.py:555
  103.9 0.2 concatenate.220
  104.2 1.6 %fusion.84 = f32[1,4,16,512]{3,0,2,1:T(1,128)S(1)} fusion(bf16[32,4,16,511]{3,0,2,1:T(8,128)(2,1)S(1)} %get-tuple-element.21, bf16[32,4,16,511]{3,0,2,1:T(8,128)(2,1)S(1)} %get-tuple-element.20, bf16[32,4,16,512]{3,0,2,1:T(8,128)(2,1)S(1)} %concatenate.220, bf16[1,32]{1,0:T(2,128)(2,1)S(1)} %get-tuple-element.68, bf16[1,32]{1,0:T(2,128)(2,1)S(1)} %get-tuple-element.69, ...), kind=kOutput, calls=%fused_computation.74 | convolution fusion | flops 37749312 | bytes 6414528 | tf_op jit(solution)/shard_map/oc,csaw->osaw/dot_general | solution.py:566
  105.8 1.3 %fusion.214 = (bf16[32,4,16,511]{3,0,2,1:T(8,128)(2,1)S(1)}, bf16[32,4,16,511]{3,0,2,1:T(8,128)(2,1)S(1)}) fusion(bf16[32,4,16,512]{3,0,2,1:T(8,128)(2,1)S(1)} %maximum_convert_fusion), kind=kLoop, calls=%fused_computation.273 | loop fusion | bytes 8372224 | tf_op jit(solution)/shard_map/slice | solution.py:555
  107.0 1.6 %fusion.86 = f32[1,4,16,512]{3,0,2,1:T(1,128)S(1)} fusion(bf16[32,4,16,511]{3,0,2,1:T(8,128)(2,1)S(1)} %get-tuple-element.9, bf16[32,4,16,511]{3,0,2,1:T(8,128)(2,1)S(1)} %get-tuple-element.8, bf16[32,4,16,512]{3,0,2,1:T(8,128)(2,1)S(1)} %maximum_convert_fusion, bf16[1,32]{1,0:T(2,128)(2,1)S(1)} %get-tuple-element.71, ...), kind=kOutput, calls=%fused_computation.75 | convolution fusion | flops 37749312 | bytes 6414528 | tf_op jit(solution)/shard_map/oc,csaw->osaw/dot_general | solution.py:566
  108.7 1.3 %pad_slice_fusion.7 = (bf16[32,4,16,511]{3,0,2,1:T(8,128)(2,1)S(1)}, bf16[32,4,16,511]{3,0,2,1:T(8,128)(2,1)S(1)}) fusion(bf16[32,4,15,512]{3,0,2,1:T(8,128)(2,1)S(1)} %get-tuple-element.6), kind=kLoop, calls=%fused_computation.263 | loop fusion | bytes 6152192 | tf_op jit(solution)/shard_map/slice | solution.py:555
  110.0 0.2 concatenate.211
  110.2 1.6 %fusion.88 = f32[1,4,16,512]{3,0,2,1:T(1,128)S(1)} fusion(bf16[32,4,16,511]{3,0,2,1:T(8,128)(2,1)S(1)} %get-tuple-element.19, bf16[32,4,16,511]{3,0,2,1:T(8,128)(2,1)S(1)} %get-tuple-element.18, bf16[32,4,16,512]{3,0,2,1:T(8,128)(2,1)S(1)} %concatenate.211, bf16[1,32]{1,0:T(2,128)(2,1)S(1)} %get-tuple-element.74, bf16[1,32]{1,0:T(2,128)(2,1)S(1)} %get-tuple-element.75, ...), kind=kOutput, calls=%fused_computation.76 | convolution fusion | flops 37749312 | bytes 6414528 | tf_op jit(solution)/shard_map/oc,csaw->osaw/dot_general | solution.py:566
  111.8 0.7 fusion.121
  112.5 0.7 copy.46
  (24 shorter events, 0.2 us)
Async XLA Ops:
  0.6 1.6 %copy-start = (f32[2,512,512]{2,1,0:T(8,128)S(1)}, f32[2,512,512]{2,1,0:T(8,128)}, u32[]{:S(2)}) copy-start(f32[2,512,512]{2,1,0:T(8,128)} %probe_hbm.1) | copy-start | bytes 6291460
  2.2 1.6 %copy-start.1 = (f32[2,1,512,512]{3,2,1,0:T(8,128)S(1)}, f32[2,1,512,512]{3,2,1,0:T(8,128)}, u32[]{:S(2)}) copy-start(f32[2,1,512,512]{3,2,1,0:T(8,128)} %amps_hbm.1) | copy-start | bytes 6291460
  3.8 0.9 copy-start.2
  4.8 0.7 copy-start.3
  5.4 1.0 copy-start.4
  6.5 1.0 copy-start.5
  7.5 72.6 %copy-start.10 = (s32[16]{0:T(128)S(1)}, s32[16]{0:T(128)}, u32[]{:S(2)}) copy-start(s32[16]{0:T(128)} %param.16) | copy-start | bytes 196
  7.5 73.2 %copy-start.8 = (bf16[3,3,32,2]{2,3,1,0:T(2,128)(2,1)S(1)}, bf16[3,3,32,2]{2,3,1,0:T(2,128)(2,1)}, u32[]{:S(2)}) copy-start(bf16[3,3,32,2]{2,3,1,0:T(2,128)(2,1)} %param.17) | copy-start | bytes 3460
  81.5 1.1 %copy-start.11 = (f32[32]{0:T(128)S(1)}, f32[32]{0:T(128)}, u32[]{:S(2)}) copy-start(f32[32]{0:T(128)} %param.18) | copy-start | bytes 388
  84.5 1.6 %copy-start.6 = (bf16[2,3,3,32,32]{4,3,2,1,0:T(8,128)(2,1)S(1)}, bf16[2,3,3,32,32]{4,3,2,1,0:T(8,128)(2,1)}, u32[]{:S(2)}) copy-start(bf16[2,3,3,32,32]{4,3,2,1,0:T(8,128)(2,1)} %param.19) | copy-start | bytes 110596
  88.7 1.0 copy-start.9
  102.6 1.6 %copy-start.7 = (bf16[3,3,32]{2,1,0:T(4,128)(2,1)S(1)}, bf16[3,3,32]{2,1,0:T(4,128)(2,1)}, u32[]{:S(2)}) copy-start(bf16[3,3,32]{2,1,0:T(4,128)(2,1)} %param.21) | copy-start | bytes 1732
where the time goes:
time: 114 us; the launch traced here: 113 us
  Pallas kernels  72.6 us (64%)
  local copies, waits for them, and re-layouts  22.5 us (20%)
  matrix products  16.1 us (14%)
    pallas_call x1, Pallas kernels, sweeps(): pl.pallas_call(main_kernel, out_shape=(jax.ShapeDtypeStruct((2,) + tile,...  72.6 us
    dot_general x12, matrix products, conv_layer(): jnp.einsum('oc,csaw->osaw', merged, stacked, preferred_element_type=jnp.f...  15.9 us
    slice x12, local copies, waits for them, and re-layouts, shift_along(): lax.slice_in_dim(values, 0, length - 1, axis=axis)  12.4 us
    unnamed x25, local copies, waits for them, and re-layouts  7.62 us

commit v1 on v0

v1 whole, which is shorter than its diff:
```python
import functools

import jax
import jax.numpy as jnp
import ml_dtypes
import numpy as np
from jax import lax
from jax.experimental import pallas as pl
from jax.experimental.pallas import tpu as pltpu
from jax.sharding import PartitionSpec as P

soften = 0.25
learning = 1.5
N = 512
B = 128
f32 = jnp.float32
bf16 = jnp.bfloat16
MESH = pl.DeviceIdType.MESH


def make_tables():
    f = np.arange(N)
    g = np.where(f < N // 2, f, f - N).astype(np.float64)
    lam = np.exp(-3j * np.pi * g * g / (4 * N))
    d = np.arange(B)[:, None] - np.arange(B)[None, :]
    blocks = []
    for m in range(4):
        fm = np.arange(m, N, 4)
        c = (lam[fm] * np.exp(2j * np.pi * fm * d[:, :, None] / N)).sum(-1) / N
        blocks.append(np.block([[c.real, -c.imag], [c.imag, c.real]]))
    left = np.stack(blocks)
    pair = np.stack([left, np.swapaxes(left, 1, 2)]).astype(ml_dtypes.bfloat16)
    orders = [np.arange(256) ^ (32 * k) for k in range(4)]
    return np.stack([pair[:, :, order][:, :, :, order] for order in orders])


def add(a, b):
    return (a[0] + b[0], a[1] + b[1])


def sub(a, b):
    return (a[0] - b[0], a[1] - b[1])


def add_i(a, b):
    return (a[0] - b[1], a[1] + b[0])


def sub_i(a, b):
    return (a[0] + b[1], a[1] - b[0])


def fold(x):
    t0, t1, t2, t3 = add(x[0], x[2]), sub(x[0], x[2]), add(x[1], x[3]), sub(x[1], x[3])
    return [add(t0, t2), sub_i(t1, t3), sub(t0, t2), add_i(t1, t3)]


def unfold(x):
    t0, t1, t2, t3 = add(x[0], x[2]), sub(x[0], x[2]), add(x[1], x[3]), sub(x[1], x[3])
    return [add(t0, t2), add_i(t1, t3), sub(t0, t2), sub_i(t1, t3)]


def fold2(e):
    rows = [fold(e[q]) for q in range(4)]
    cols = [fold([rows[q][m] for q in range(4)]) for m in range(4)]
    return [[cols[mc][mr] for mc in range(4)] for mr in range(4)]


def unfold2(e):
    cols = [unfold([e[q][m] for q in range(4)]) for m in range(4)]
    return [unfold([cols[m][q] for m in range(4)]) for q in range(4)]


def lanes(q):
    return slice(q * B, q * B + B)


def store_y(ya, y, row, n):
    for mr in range(4):
        for mc in range(4):
            for ri in range(2):
                at = (mr * 2 + ri) * B + row
                ya[at : at + n, lanes(mc)] = y[mr][mc][ri].astype(bf16)


def load_f(f, row, n):
    return [
        [
            tuple(
                f[(mr * 2 + ri) * B + row : (mr * 2 + ri) * B + row + n, lanes(mc)]
                for ri in range(2)
            )
            for mc in range(4)
        ]
        for mr in range(4)
    ]


ROWS = 16


def stage1(v, pr, ya, tile, place):
    n = ROWS
    for i in range(2):
        for part in range(0, 32, n):
            row = place * 32 + part
            e = []
            for q in range(4):
                line = []
                for c in range(4):
                    vr = v[q * 4 + tile, 0, part : part + n, lanes(c)].astype(f32)
                    vi = v[q * 4 + tile, 1, part : part + n, lanes(c)].astype(f32)
                    a = pr[i, 0, q * B + row : q * B + row + n, lanes(c)].astype(f32)
                    b = pr[i, 1, q * B + row : q * B + row + n, lanes(c)].astype(f32)
                    line.append((a * vr - b * vi, a * vi + b * vr))
                e.append(line)
            store_y(ya.at[i], fold2(e), row, n)


def right(ya, mats, out, dtype, place):
    rows = [(i, slice(m * B + place * 32, m * B + place * 32 + 32)) for i in range(2) for m in range(8)]
    for mc in range(4):
        lhs = jnp.concatenate(
            [
                jnp.concatenate([ya[i, at, lanes(mc)] for i, at in rows[p : p + 2]], 1)
                for p in range(0, 16, 2)
            ],
            0,
        )
        r = jnp.dot(lhs, mats[mc], preferred_element_type=f32)
        for p, (i, at) in enumerate(rows):
            out[i, at, lanes(mc)] = r[p // 2 * 32 : p // 2 * 32 + 32, lanes(p % 2)].astype(dtype)


def left_part(mats, yb, out, dtype, mr):
    at = slice(mr * 256, mr * 256 + 256)
    out[at, :] = jnp.dot(mats[mr], yb[at, :], preferred_element_type=f32).astype(dtype)


def stage2_part(f, am, ya, g):
    n = ROWS
    row = g * n
    w = unfold2(load_f(f, row, n))
    for q in range(4):
        for c in range(4):
            wr, wi = w[q][c]
            a = am[q * B + row : q * B + row + n, lanes(c)].astype(f32)
            s = 1.0 - a * lax.rsqrt(wr * wr + wi * wi + soften)
            w[q][c] = (wr * s, wi * s)
    store_y(ya, fold2(w), row, n)


def middle(mat_l, mat_r, am, ya, yb, ff, before_second):
    def lead(i, g):
        left_part(mat_l, yb.at[i], ff.at[i], f32, g)

    def back(i, g):
        left_part(mat_r, ya.at[i], yb.at[i], bf16, g)

    def misfit(i, g):
        for h in (2 * g, 2 * g + 1):
            stage2_part(ff.at[i], am.at[i], ya.at[i], h)

    for g in range(4):
        lead(0, g)
    for g in range(4):
        lead(1, g)
        misfit(0, g)
    before_second()
    for g in range(4):
        back(0, g)
        misfit(1, g)
    for g in range(4):
        back(1, g)


def stage3(f, pr, g, place):
    n = ROWS
    for part in range(0, 32, n):
        row = place * 32 + part
        tot = None
        for i in range(2):
            w = unfold2(load_f(f.at[i], row, n))
            new = []
            for q in range(4):
                for c in range(4):
                    a = pr[i, 0, q * B + row : q * B + row + n, lanes(c)].astype(f32)
                    b = pr[i, 1, q * B + row : q * B + row + n, lanes(c)].astype(f32)
                    br, bi = w[q][c]
                    new.append((a * br + b * bi, a * bi - b * br))
            tot = new if tot is None else [add(p, q) for p, q in zip(tot, new)]
        for q in range(4):
            for c in range(4):
                for ri in range(2):
                    g[q, ri, part : part + n, lanes(c)] = tot[q * 4 + c][ri].astype(g.dtype)


def one_hot(offset, order, transpose):
    a = lax.broadcasted_iota(jnp.int32, (N, N), 0)
    b = lax.broadcasted_iota(jnp.int32, (N, N), 1)
    if transpose:
        return jnp.where(a == ((b + offset) & (N - 1)), 1.0, 0.0).astype(bf16)
    return jnp.where(b == (((a ^ order) + offset) & (N - 1)), 1.0, 0.0).astype(bf16)


def make_hot(off, order, hot):
    hot[0] = one_hot(off[0:1, 0:1], order, False)
    hot[1] = one_hot(off[8:9, 0:1], order, True)


def roll_plane(src, hot, tmp, dst):
    for h in range(2):
        sl = slice(h * 256, h * 256 + 256)
        tmp[sl, :] = jnp.dot(hot[0, sl, :], src[...], preferred_element_type=f32).astype(bf16)
    for h in range(2):
        sl = slice(h * 256, h * 256 + 256)
        dst[sl, :] = jnp.dot(tmp[sl, :], hot[1], preferred_element_type=f32).astype(bf16)


SEG = 320
DEPTH = 3 * SEG


def net_weights(conv_first, bias_first, conv_middle, bias_middle, conv_last, pad, w_first, w_mid, w_last, bias):
    pad[...] = jnp.zeros_like(pad)
    for layer in range(2):
        for p in range(3):
            for t in range(3):
                pad[p * 3 + t, :, 0:32] = conv_middle[layer, p, t].astype(f32)
        turned = [
            [[pltpu.roll(pad[p * 3 + t], 32 * m, 1) if m else pad[p * 3 + t] for m in range(4)] for t in range(3)]
            for p in range(3)
        ]
        for k in range(8):
            blocks = [None] * 8
            for t in range(3):
                for p in range(3):
                    at = t * SEG + (k + p) * 32
                    piece = turned[p][t][at // 32 % 4]
                    held = blocks[at // B]
                    blocks[at // B] = piece if held is None else held + piece
            for j in range(8):
                value = jnp.zeros((32, B), f32) if blocks[j] is None else blocks[j]
                w_mid[layer, k * 32 : k * 32 + 32, lanes(j)] = value.astype(bf16)
    pad[...] = jnp.zeros_like(pad)
    square = pad.at[0:4]
    for p in range(3):
        for t in range(3):
            at = (p * 3 + t) * 8
            square[at // 32, at % 32 : at % 32 + 2, 0:32] = conv_first[p, t].astype(f32)
    flipped = jnp.transpose(pad[0:4].reshape(B, B))[0:32, :]
    group = lax.broadcasted_iota(jnp.int32, (32, B), 1) >> 3
    base = jnp.zeros((32, 256), f32)
    for p in range(3):
        for t in range(3):
            piece = jnp.where(group == p * 3 + t, flipped, 0.0)
            wide = jnp.concatenate([piece, jnp.zeros((32, B), f32)], 1)
            base = base + pltpu.roll(wide, (t * 48 + 6 + 2 * p - (p * 3 + t) * 8) % 256, 1)
    for k in range(16):
        w_first[k * 32 : k * 32 + 32, :] = (pltpu.roll(base, 2 * k, 1) if k else base).astype(bf16)
    pad[...] = jnp.zeros_like(pad)
    base = jnp.zeros((8, 640), f32)
    for p in range(3):
        pad[p, 0:3, 0:32] = conv_last[p].astype(f32)
        wide = jnp.concatenate([pad[p, 0:8, :], jnp.zeros((8, 512), f32)], 1)
        base = base + (pltpu.roll(wide, 32 * p, 1) if p else wide)
    row = lax.broadcasted_iota(jnp.int32, (16, N), 0)
    taps = [jnp.zeros((16, N), f32) for t in range(3)]
    for k in range(16):
        turned_k = (pltpu.roll(base, (32 * (k - 1)) % 640, 1) if k != 1 else base)[:, 0:N]
        for t in range(3):
            taps[t] = jnp.where(row == k, jnp.broadcast_to(turned_k[t : t + 1, :], (16, N)), taps[t])
    for t in range(3):
        w_last[t * 16 : t * 16 + 16, :] = taps[t].astype(bf16)
    eye = lax.broadcasted_iota(jnp.int32, (32, 32), 0) == lax.broadcasted_iota(jnp.int32, (32, 32), 1)
    for i in range(3):
        line = bias_first[0:1, :] if i == 0 else bias_middle[i - 1 : i, :]
        column = jnp.sum(jnp.where(eye, jnp.broadcast_to(line, (32, 32)), 0.0), axis=1, keepdims=True)
        bias[i] = jnp.broadcast_to(column, (32, B))


def make_perm(slot_angle, perm):
    r = lax.broadcasted_iota(jnp.int32, (B, B), 0)
    m = lax.broadcasted_iota(jnp.int32, (B, B), 1)
    angle = jnp.zeros((B, B), jnp.int32)
    for j in range(16):
        angle = jnp.where((m >> 3) == j, slot_angle[j], angle)
    hit = ((r >> 5) == (m & 3)) & ((r & 1) == ((m >> 2) & 1)) & (((r >> 1) & 15) == angle)
    perm[...] = jnp.where(hit, 1.0, 0.0).astype(bf16)


def taps_of(value):
    width = value.shape[1]
    lane = lax.broadcasted_iota(jnp.int32, value.shape, 1)
    before = jnp.where(lane == 0, 0.0, pltpu.roll(value, 1, 1))
    after = jnp.where(lane == width - 1, 0.0, pltpu.roll(value, width - 1, 1))
    return before, value, after


def net_layer_out(out, bias_i, b, u, dst, last):
    for k in range(8):
        block = jnp.concatenate(
            [jnp.maximum(out[k * 32 : k * 32 + 32, lanes(q)] + bias_i, 0.0) for q in range(4)], 1
        )
        if last:
            dst[u, (b * 8 + k) * 32 : (b * 8 + k) * 32 + 32, :] = block.astype(bf16)
            continue
        for t, piece in enumerate(taps_of(block)):
            piece = piece.astype(bf16)
            at = t * SEG + (k + 1) * 32
            dst[u, b, at : at + 32, :] = piece
            if b == 0 and k == 7:
                dst[u, 1, t * SEG : t * SEG + 32, :] = piece
            if b == 1 and k == 0:
                dst[u, 0, t * SEG + 288 : t * SEG + 320, :] = piece


def net_clear(ha, hb):
    for h in (ha, hb):
        for u in range(4):
            for t in range(3):
                zero = jnp.zeros((32, N), bf16)
                h[u, 0, t * SEG : t * SEG + 32, :] = zero
                h[u, 1, t * SEG + 288 : t * SEG + 320, :] = zero
            for b in range(2):
                h[u, b, DEPTH:1024, :] = jnp.zeros((1024 - DEPTH, N), bf16)


def net_run(nb, perm, w_first, w_mid, w_last, bias, ordered, ha, hb, hc, out_ref):
    ordered[...] = jnp.dot(perm[...], nb[...].reshape(B, N), preferred_element_type=f32)

    def first(u, _):
        mine = ordered[pl.ds(pl.multiple_of(u * 32, 32), 32), :]
        zero = jnp.zeros((8, N), f32)
        parts = []
        for piece in taps_of(mine):
            parts += [zero, piece, zero]
        stacked = jnp.concatenate(parts + [jnp.zeros((256 - 144, N), f32)], 0).astype(bf16)
        for b in range(2):
            out = jnp.dot(w_first[b * 256 : b * 256 + 256, :], stacked, preferred_element_type=f32)
            net_layer_out(out, bias[0], b, u, ha, False)
        return 0

    lax.fori_loop(0, 4, first, 0)
    for layer in range(2):
        src, dst = (ha, hb) if layer == 0 else (hb, hc)

        def middle(u, _):
            for b in range(2):
                out = jnp.dot(w_mid[layer], src[u, b], preferred_element_type=f32)
                net_layer_out(out, bias[layer + 1], b, u, dst, layer == 1)
            return 0

        lax.fori_loop(0, 4, middle, 0)

    def final(u, _):
        out = jnp.dot(w_last[...], hc[u], preferred_element_type=f32)
        before = taps_of(out[0:16, :])[0]
        after = taps_of(out[32:48, :])[2]
        at = pl.multiple_of(128 + u * 16, 16)
        out_ref[pl.ds(at, 16), :] = before + out[16:32, :] + after
        return 0

    lax.fori_loop(0, 4, final, 0)


def main_kernel(
    obj,
    probe_hbm,
    amps_hbm,
    off,
    mats_hbm,
    slot_angle,
    conv_first,
    bias_first,
    conv_middle,
    bias_middle,
    conv_last,
    out,
    mats,
    pad,
    w_first,
    w_mid,
    w_last,
    bias,
    perm,
    ordered,
    ha,
    hb,
    hc,
    view,
    probe_in,
    amps_in,
    probe16,
    amp16,
    amp_send,
    amp_recv,
    off_own,
    off_send,
    off_recv,
    hot,
    tmp,
    pr,
    am,
    ya,
    yb,
    ff,
    x_obj,
    g_send,
    g_recv,
    g_own,
    sa,
    sb,
    ra,
    rb,
    total,
    as_send,
    nb,
    local_sem,
    x_sem,
    ag_recv,
    ring_send,
    sib_send,
    gs_sem,
    gr_sem,
    sa_sem,
    sb_sem,
    ra_sem,
    rb_sem,
    aa_send,
    aa_recv,
):
    pos = lax.axis_index("pos")
    ang = lax.axis_index("ang")
    c = lax.rem(pos, 2)
    s = lax.rem(pos // 2, 2)
    y = pos // 4
    me = 2 * s + c
    up = lax.rem(y + 1, 4)
    down = lax.rem(y + 3, 4)
    far = lax.rem(y + 2, 4)

    def at(yy, xx, cc):
        return yy * 4 + xx * 2 + cc

    dev_up = (ang, at(up, s, c))
    dev_down = (ang, at(down, s, c))
    dev_far = (ang, at(far, s, c))
    dev_x = (ang, at(y, 1 - s, c))
    dev_sib = (ang, at(y, s, 1 - c))
    step_size = learning / 16

    def put_obj(slot, value):
        for ri in range(2):
            out[pl.ds(pl.multiple_of(slot * 64 + ri * 32, 32), 32), :] = value[ri]

    def rc(src, dst, send, recv, dev):
        return pltpu.make_async_remote_copy(
            src_ref=src, dst_ref=dst, send_sem=send, recv_sem=recv, device_id=dev,
            device_id_type=MESH,
        )

    def arrived(dst, recv):
        rc(dst, dst, recv, recv, dev_x).wait_recv()

    def left_dev(src, send):
        rc(src, src, send, send, dev_x).wait_send()

    cp_probe = pltpu.make_async_copy(probe_hbm, probe_in, local_sem.at[0])
    cp_amps = pltpu.make_async_copy(amps_hbm, amps_in, local_sem.at[1])
    cp_mats = pltpu.make_async_copy(mats_hbm.at[0], mats.at[0], local_sem.at[2])
    cp_mats_mine = pltpu.make_async_copy(mats_hbm.at[me], mats.at[1], local_sem.at[3])
    cp_amps.start()
    cp_probe.start()
    cp_mats.start()
    cp_mats_mine.start()
    mat_l, mat_r = mats.at[0, 0], mats.at[0, 1]
    row_l, row_r = mats.at[1, 0], mats.at[1, 1]

    barrier = pltpu.get_barrier_semaphore()
    peers = [dev_up, dev_down, dev_far, dev_x, dev_sib]
    peers += [(ang, at(yy, 1 - s, c)) for yy in (up, down, far)]
    for dev in peers:
        pl.semaphore_signal(barrier, inc=1, device_id=dev, device_id_type=MESH)
    for d in range(1, 8):
        pl.semaphore_signal(
            barrier, inc=1, device_id=(lax.rem(ang + d, 8), pos), device_id_type=MESH
        )

    own = at(y, s, c)
    other = at(y, 1 - s, c)
    view[0, own] = obj[s].astype(bf16)
    x_obj[...] = obj[1 - s].astype(bf16)
    for i, (ref, slot) in enumerate(((off_own, s), (off_send, 1 - s))):
        for k in range(2):
            value = jnp.where(slot == 0, off[0, 0, k], off[1, 0, k])
            ref[k * 8 : k * 8 + 8, :] = jnp.full((8, 128), value, jnp.int32)

    pl.semaphore_wait(barrier, 15)

    rc(x_obj, view.at[0, own], x_sem.at[0], ag_recv.at[0, own], dev_x).start()
    rc(off_send, off_recv, x_sem.at[1], x_sem.at[2], dev_x).start()

    around = ((up, dev_up), (down, dev_down), (far, dev_far))

    def ag_start(k, xx):
        tile = at(y, xx, c)
        ref = view.at[k, tile]
        for d, (_, dev) in enumerate(around):
            rc(ref, ref, ring_send.at[k, xx, d], ag_recv.at[k, tile], dev).start()
        rc(ref, ref, sib_send.at[k, 3, xx], ag_recv.at[k, tile], dev_sib).start()

    def ag_relay(k, xx):
        for d, (yy, _) in enumerate(around):
            tile = at(yy, xx, c)
            ref = view.at[k, tile]
            arrived(ref, ag_recv.at[k, tile])
            rc(ref, ref, sib_send.at[k, d, xx], ag_recv.at[k, tile], dev_sib).start()

    def ag_rest(k, xx):
        for yy in range(4):
            tile = at(yy, xx, 1 - c)
            arrived(view.at[k, tile], ag_recv.at[k, tile])

    def ag_sent(k):
        for xx in range(2):
            tile = at(y, xx, c)
            for d in range(3):
                left_dev(view.at[k, tile], ring_send.at[k, xx, d])
            for d, yy in enumerate((up, down, far, y)):
                left_dev(view.at[k, at(yy, xx, c)], sib_send.at[k, d, xx])

    ag_start(0, s)
    cp_amps.wait()
    amp_send[...] = amps_in[1 - s, 0].astype(bf16)
    cp_amp_x = rc(amp_send, amp_recv, x_sem.at[3], x_sem.at[4], dev_x)
    cp_amp_x.start()
    amp16[...] = amps_in[s, 0].astype(bf16)
    arrived(view.at[0, other], ag_recv.at[0, other])
    ag_start(0, 1 - s)
    cp_probe.wait()
    probe16[...] = probe_in[...].astype(bf16)
    make_hot(off_own, 32 * me, hot.at[0])
    roll_plane(probe16.at[0], hot.at[0], tmp, pr.at[0, 0])
    roll_plane(probe16.at[1], hot.at[0], tmp, pr.at[0, 1])
    ag_relay(0, s)
    arrived(off_recv, x_sem.at[2])
    make_hot(off_recv, 32 * me, hot.at[1])
    roll_plane(probe16.at[0], hot.at[1], tmp, pr.at[1, 0])
    ag_relay(0, 1 - s)
    roll_plane(probe16.at[1], hot.at[1], tmp, pr.at[1, 1])
    cp_mats.wait()
    cp_mats_mine.wait()

    cols = (s, 1 - s)
    tiles = (me, 2 * s + 1 - c, 2 * (1 - s) + c, 2 * (1 - s) + 1 - c)

    def enter(k, *places):
        for place in places:
            stage1(view.at[k], pr, ya, tiles[place], place)
        for place in places:
            right(ya, mat_r, yb, bf16, place)

    def leave(g, place):
        right(yb, mat_l, ff, f32, place)
        stage3(ff, pr, g, place)

    def before_second(k):
        if k == 0:
            arrived(amp_recv, x_sem.at[4])
            roll_plane(amp_recv, hot.at[1], tmp, am.at[1])

    for k in range(2):
        if k == 1:
            ag_relay(k, s)
        enter(k, 0)
        if k == 1:
            ag_relay(k, 1 - s)
        ag_rest(k, s)
        enter(k, 1, 2)
        ag_rest(k, 1 - s)
        enter(k, 3)
        if k == 0:
            roll_plane(amp16, hot.at[0], tmp, am.at[0])
        middle(row_l, row_r, am, ya, yb, ff, functools.partial(before_second, k))
        order = (0, 1) if k == 0 else (1, 0)
        for o in order:
            leave(g_send.at[k, o], 2 * o + 1)
            rc(g_send.at[k, o], g_recv.at[k, o], gs_sem.at[k, o], gr_sem.at[k, o],
               dev_sib).start()

        def comb(yy, o):
            return g_own[o, yy] + g_recv[k, o, yy].astype(f32)

        if k == 0:
            for o in order:
                leave(g_own.at[o], 2 * o)
                arrived(g_recv.at[0, o], gr_sem.at[0, o])
                for d, (yy, dev) in ((2, around[2]), (0, around[0]), (1, around[1])):
                    sa[d, o] = comb(yy, o).astype(bf16)
                    rc(sa.at[d, o], ra.at[d, o], sa_sem.at[d, o], ra_sem.at[d, o], dev).start()
            ag_sent(0)
            net_weights(
                conv_first, bias_first, conv_middle, bias_middle, conv_last, pad, w_first, w_mid,
                w_last, bias,
            )
            for o in order:
                sum_x = comb(y, o)
                for d in range(3):
                    arrived(ra.at[d, o], ra_sem.at[d, o])
                    sum_x = sum_x + ra[d, o].astype(f32)
                total[o] = sum_x
                if o == 0:
                    view[1, own] = (obj[s] - step_size * sum_x).astype(bf16)
                else:
                    view[1, other] = (view[0, other].astype(f32) - step_size * sum_x).astype(bf16)
                ag_start(1, cols[o])
            make_perm(slot_angle, perm)
            net_clear(ha, hb)
            for d in range(3):
                for o in range(2):
                    left_dev(sa.at[d, o], sa_sem.at[d, o])
        else:
            for o in order:
                leave(g_own.at[o], 2 * o)
                arrived(g_recv.at[1, o], gr_sem.at[1, o])
                if o == 1:
                    sb[1, 3] = (comb(y, 1) + total[1]).astype(bf16)
                    rc(sb.at[1, 3], rb.at[1, 3], sb_sem.at[1, 3], rb_sem.at[1, 3], dev_x).start()
                for d, (yy, _) in ((2, around[2]), (0, around[0]), (1, around[1])):
                    sb[o, d] = comb(yy, o).astype(bf16)
                    rc(sb.at[o, d], rb.at[o, d], sb_sem.at[o, d], rb_sem.at[o, d],
                       (ang, at(yy, cols[o], c))).start()
            ag_sent(1)
            for d in range(4):
                arrived(rb.at[1, d], rb_sem.at[1, d])
            theirs = (
                rb[1, 0].astype(f32) + rb[1, 1].astype(f32) + rb[1, 2].astype(f32)
                + rb[1, 3].astype(f32)
            )
            put_obj(1 - s, obj[1 - s] - step_size * theirs)
            mine = comb(y, 0) + total[0]
            for d in range(3):
                arrived(rb.at[0, d], rb_sem.at[0, d])
                mine = mine + rb[0, d].astype(f32)
            put_obj(s, obj[s] - step_size * mine)
        for o in range(2):
            left_dev(g_send.at[k, o], gs_sem.at[k, o])

    for g in range(8):
        as_send[g] = jnp.concatenate(
            [out[q * 32 + g * 4 : q * 32 + g * 4 + 4, :] for q in range(4)], 0
        ).astype(bf16)

    def a2a(d):
        to = lax.rem(ang + d, 8)
        return rc(as_send.at[to], nb.at[ang], aa_send.at[d], aa_recv.at[ang], (to, pos))

    for d in range(1, 8):
        a2a(d).start()
    nb[ang] = as_send[ang]
    for d in range(1, 8):
        frm = lax.rem(ang + d, 8)
        arrived(nb.at[frm], aa_recv.at[frm])
    net_run(nb, perm, w_first, w_mid, w_last, bias, ordered, ha, hb, hc, out)
    for d in range(1, 8):
        a2a(d).wait_send()
    for o in range(2):
        for d in range(3 + o):
            left_dev(sb.at[o, d], sb_sem.at[o, d])
    left_dev(x_obj, x_sem.at[0])
    left_dev(off_send, x_sem.at[1])
    cp_amp_x.wait_send()


def split_kernel(both, obj_out, proj_out):
    obj_out[...] = both[0:128]
    proj_out[...] = both[128:192]


def split(both):
    vm = pl.BlockSpec(memory_space=pltpu.VMEM)
    return pl.pallas_call(
        split_kernel,
        out_shape=(
            jax.ShapeDtypeStruct((128, N), f32),
            jax.ShapeDtypeStruct((64, N), f32),
        ),
        in_specs=[vm],
        out_specs=(vm, vm),
    )(both)


def sweeps(
    object_init,
    probe_field,
    amplitudes,
    offsets,
    slot_angle,
    conv_first,
    bias_first,
    conv_middle,
    bias_middle,
    conv_last,
):
    mats = make_tables()
    vm = pl.BlockSpec(memory_space=pltpu.VMEM)
    hbm = pl.BlockSpec(memory_space=pltpu.HBM)
    smem = pl.BlockSpec(memory_space=pltpu.SMEM)
    tile = (2, 32, N)
    scratch = [
        pltpu.VMEM((2, 2, 4, 256, 256), bf16),
        pltpu.VMEM((9, 32, B), f32),
        pltpu.VMEM((N, 256), bf16),
        pltpu.VMEM((2, 256, 1024), bf16),
        pltpu.VMEM((48, N), bf16),
        pltpu.VMEM((3, 32, B), f32),
        pltpu.VMEM((B, B), bf16),
        pltpu.VMEM((B, N), f32),
        pltpu.VMEM((4, 2, 1024, N), bf16),
        pltpu.VMEM((4, 2, 1024, N), bf16),
        pltpu.VMEM((4, N, N), bf16),
        pltpu.VMEM((2, 16) + tile, bf16),
        pltpu.VMEM((2, N, N), f32),
        pltpu.VMEM((2, 1, N, N), f32),
        pltpu.VMEM((2, N, N), bf16),
        pltpu.VMEM((N, N), bf16),
        pltpu.VMEM((N, N), bf16),
        pltpu.VMEM((N, N), bf16),
        pltpu.VMEM((16, 128), jnp.int32),
        pltpu.VMEM((16, 128), jnp.int32),
        pltpu.VMEM((16, 128), jnp.int32),
        pltpu.VMEM((2, 2, N, N), bf16),
        pltpu.VMEM((N, N), bf16),
        pltpu.VMEM((2, 2, N, N), bf16),
        pltpu.VMEM((2, N, N), bf16),
        pltpu.VMEM((2, 2 * N, N), bf16),
        pltpu.VMEM((2, 2 * N, N), bf16),
        pltpu.VMEM((2, 2 * N, N), f32),
        pltpu.VMEM(tile, bf16),
        pltpu.VMEM((2, 2, 4) + tile, bf16),
        pltpu.VMEM((2, 2, 4) + tile, bf16),
        pltpu.VMEM((2, 4) + tile, f32),
        pltpu.VMEM((3, 2) + tile, bf16),
        pltpu.VMEM((2, 4) + tile, bf16),
        pltpu.VMEM((3, 2) + tile, bf16),
        pltpu.VMEM((2, 4) + tile, bf16),
        pltpu.VMEM((2,) + tile, f32),
        pltpu.VMEM((8, 16, N), bf16),
        pltpu.VMEM((8, 16, N), bf16),
        pltpu.SemaphoreType.DMA((4,)),
        pltpu.SemaphoreType.DMA((5,)),
        pltpu.SemaphoreType.DMA((2, 16)),
        pltpu.SemaphoreType.DMA((2, 2, 3)),
        pltpu.SemaphoreType.DMA((2, 4, 2)),
        pltpu.SemaphoreType.DMA((2, 2)),
        pltpu.SemaphoreType.DMA((2, 2)),
        pltpu.SemaphoreType.DMA((3, 2)),
        pltpu.SemaphoreType.DMA((2, 4)),
        pltpu.SemaphoreType.DMA((3, 2)),
        pltpu.SemaphoreType.DMA((2, 4)),
        pltpu.SemaphoreType.DMA((8,)),
        pltpu.SemaphoreType.DMA((8,)),
    ]
    return pl.pallas_call(
        main_kernel,
        out_shape=jax.ShapeDtypeStruct((192, N), f32),
        in_specs=[vm, hbm, hbm, smem, hbm, smem] + [vm] * 5,
        out_specs=vm,
        scratch_shapes=scratch,
        compiler_params=pltpu.CompilerParams(
            collective_id=0, has_side_effects=True, vmem_limit_bytes=60 << 20
        ),
        cost_estimate=pl.CostEstimate(
            flops=12_000_000_000, bytes_accessed=8_000_000, transcendentals=1_000_000
        ),
    )(
        object_init,
        probe_field,
        amplitudes,
        offsets,
        jnp.asarray(mats),
        slot_angle,
        conv_first.transpose(0, 1, 3, 2),
        bias_first.reshape(1, 32),
        conv_middle,
        bias_middle,
        conv_last,
    )


def on_device(
    object_init,
    probe_field,
    amplitudes,
    offsets,
    slot_angle,
    conv_first,
    bias_first,
    conv_middle,
    bias_middle,
    conv_last,
):
    both = sweeps(
        object_init,
        probe_field,
        amplitudes,
        offsets,
        slot_angle,
        conv_first,
        bias_first,
        conv_middle,
        bias_middle,
        conv_last,
    )
    obj_new, projections = split(both)
    return (obj_new.reshape(2, 2, 32, N), projections.reshape(1, 1, 4, 16, N))


def solution(mesh):
    return jax.shard_map(
        on_device,
        mesh=mesh,
        in_specs=(
            P("ang", None, "pos", None),
            P(),
            P("ang", "pos", None, None),
            P("ang", "pos", None),
            P(),
            P(),
            P(),
            P(),
            P(),
            P(),
        ),
        out_specs=(P("ang", None, "pos", None), P("pos", "ang", None, None, None)),
        check_vma=False,
    )
```

time: 114 us -> 76.4 us (0.67)
  local copies, waits for them, and re-layouts: 22.5 us -> 0 us
  matrix products: 16.1 us -> 0 us
  Pallas kernels: 72.6 us -> 75.5 us
    dot_general x13 -> x0, matrix products: 16.1 us -> none  [the longest x12 15.9 us: conv_layer(): jnp.einsum('oc,csaw->osaw', merged, stacked, preferred_element_type=jnp.f...]
    slice x15 -> x0, local copies, waits for them, and re-layouts: 13.5 us -> none  [the longest x12 12.4 us: shift_along(): lax.slice_in_dim(values, 0, length - 1, axis=axis)]
    unnamed x25 -> x0, local copies, waits for them, and re-layouts: 7.62 us -> none
    pallas_call x1 -> x2, Pallas kernels: 72.6 us -> 75.5 us  [the longest x1 73.8 us: sweeps(): pl.pallas_call(main_kernel, out_shape=jax.ShapeDtypeStruct((192, N), f32)...]
    concatenate x8 -> x0, local copies, waits for them, and re-layouts: 1.33 us -> none  [the longest x4 0.73 us: shift_along(): jnp.concatenate([padding, lax.slice_in_dim(values, 0, length - 1, axis=ax...]
where the time goes in v1:
time: 76.4 us; the launch traced here: 76.2 us
  Pallas kernels  75.5 us (99%)
    pallas_call x1, Pallas kernels, sweeps(): pl.pallas_call(main_kernel, out_shape=jax.ShapeDtypeStruct((192, N), f32)...  73.8 us
    pallas_call x1, Pallas kernels, split(): pl.pallas_call(split_kernel, out_shape=(jax.ShapeDtypeStruct((128, N), f3...  1.76 us

profile of v1, /device:TPU:0, one launch (start us, length us, event | category | flops | bytes accessed | tf_op | source)
XLA Modules:
  0.0 76.2 jit_solution(7831213840886021377)
XLA Ops:
  0.6 73.8 %shard_map.122.both = f32[192,512]{1,0:T(8,128)} custom-call(f32[2,2,32,512]{3,2,1,0:T(8,128)} %obj.1, f32[2,512,512]{2,1,0:T(8,128)} %probe_hbm.1, f32[2,1,512,512]{3,2,1,0:T(8,128)} %amps_hbm.1, s32[2,1,2]{2,1,0:T(1,128)} %off.1, bf16[4,2,4,256,256]{4,3,2,1,0:T(8,128)(2,1)} %constant.2.clone.mats_hbm, s32[16]{0:T(128)} %slot_angle.1, ...), custom_call_target="tpu_custom_call" | custom-call | flops 12000000000 | bytes 8000000 | tf_op jit(solution)/shard_map/pallas_call | solution.py:765
  74.4 1.8 %shard_map.123 = (f32[128,512]{1,0:T(8,128)}, f32[64,512]{1,0:T(8,128)}) custom-call(f32[192,512]{1,0:T(8,128)} %shard_map.122.both), custom_call_target="tpu_custom_call" | custom-call | tf_op jit(solution)/shard_map/pallas_call | solution.py:683

commit v2 on v1

--- a/solution.py
+++ b/solution.py
@@ -329,39 +329,26 @@
 def net_run(nb, perm, w_first, w_mid, w_last, bias, ordered, ha, hb, hc, out_ref):
     ordered[...] = jnp.dot(perm[...], nb[...].reshape(B, N), preferred_element_type=f32)
 
-    def first(u, _):
-        mine = ordered[pl.ds(pl.multiple_of(u * 32, 32), 32), :]
+    for u in range(4):
         zero = jnp.zeros((8, N), f32)
         parts = []
-        for piece in taps_of(mine):
+        for piece in taps_of(ordered[u * 32 : u * 32 + 32, :]):
             parts += [zero, piece, zero]
         stacked = jnp.concatenate(parts + [jnp.zeros((256 - 144, N), f32)], 0).astype(bf16)
         for b in range(2):
             out = jnp.dot(w_first[b * 256 : b * 256 + 256, :], stacked, preferred_element_type=f32)
             net_layer_out(out, bias[0], b, u, ha, False)
-        return 0
-
-    lax.fori_loop(0, 4, first, 0)
     for layer in range(2):
         src, dst = (ha, hb) if layer == 0 else (hb, hc)
-
-        def middle(u, _):
+        for u in range(4):
             for b in range(2):
                 out = jnp.dot(w_mid[layer], src[u, b], preferred_element_type=f32)
                 net_layer_out(out, bias[layer + 1], b, u, dst, layer == 1)
-            return 0
-
-        lax.fori_loop(0, 4, middle, 0)
-
-    def final(u, _):
+    for u in range(4):
         out = jnp.dot(w_last[...], hc[u], preferred_element_type=f32)
         before = taps_of(out[0:16, :])[0]
         after = taps_of(out[32:48, :])[2]
-        at = pl.multiple_of(128 + u * 16, 16)
-        out_ref[pl.ds(at, 16), :] = before + out[16:32, :] + after
-        return 0
-
-    lax.fori_loop(0, 4, final, 0)
+        out_ref[128 + u * 16 : 144 + u * 16, :] = before + out[16:32, :] + after
 
 
 def main_kernel(
@@ -578,10 +565,10 @@
             ag_relay(k, 1 - s)
         ag_rest(k, s)
         enter(k, 1, 2)
+        if k == 0:
+            roll_plane(amp16, hot.at[0], tmp, am.at[0])
         ag_rest(k, 1 - s)
         enter(k, 3)
-        if k == 0:
-            roll_plane(amp16, hot.at[0], tmp, am.at[0])
         middle(row_l, row_r, am, ya, yb, ff, functools.partial(before_second, k))
         order = (0, 1) if k == 0 else (1, 0)
         for o in order:

time: 76.4 us -> 72.7 us (0.952)
  Pallas kernels: 75.5 us -> 71.9 us
    pallas_call x1, Pallas kernels: 73.8 us -> 70.1 us  [sweeps(): pl.pallas_call(main_kernel, out_shape=jax.ShapeDtypeStruct((192, N), f32)...]
where the time goes in v2:
time: 72.7 us; the launch traced here: 72.5 us
  Pallas kernels  71.9 us (99%)
    pallas_call x1, Pallas kernels, sweeps(): pl.pallas_call(main_kernel, out_shape=jax.ShapeDtypeStruct((192, N), f32)...  70.1 us
    pallas_call x1, Pallas kernels, split(): pl.pallas_call(split_kernel, out_shape=(jax.ShapeDtypeStruct((128, N), f3...  1.76 us

profile of v2, /device:TPU:0, one launch (start us, length us, event | category | flops | bytes accessed | tf_op | source)
XLA Modules:
  0.0 72.5 jit_solution(4551543201855405522)
XLA Ops:
  0.6 70.1 %shard_map.122.both = f32[192,512]{1,0:T(8,128)} custom-call(f32[2,2,32,512]{3,2,1,0:T(8,128)} %obj.1, f32[2,512,512]{2,1,0:T(8,128)} %probe_hbm.1, f32[2,1,512,512]{3,2,1,0:T(8,128)} %amps_hbm.1, s32[2,1,2]{2,1,0:T(1,128)} %off.1, bf16[4,2,4,256,256]{4,3,2,1,0:T(8,128)(2,1)} %constant.2.clone.mats_hbm, s32[16]{0:T(128)} %slot_angle.1, ...), custom_call_target="tpu_custom_call" | custom-call | flops 12000000000 | bytes 8000000 | tf_op jit(solution)/shard_map/pallas_call | solution.py:752
  70.8 1.8 %shard_map.123 = (f32[128,512]{1,0:T(8,128)}, f32[64,512]{1,0:T(8,128)}) custom-call(f32[192,512]{1,0:T(8,128)} %shard_map.122.both), custom_call_target="tpu_custom_call" | custom-call | tf_op jit(solution)/shard_map/pallas_call | solution.py:670

commit v3 on v2

--- a/solution.py
+++ b/solution.py
@@ -340,10 +340,14 @@
             net_layer_out(out, bias[0], b, u, ha, False)
     for layer in range(2):
         src, dst = (ha, hb) if layer == 0 else (hb, hc)
+        held = None
         for u in range(4):
             for b in range(2):
                 out = jnp.dot(w_mid[layer], src[u, b], preferred_element_type=f32)
-                net_layer_out(out, bias[layer + 1], b, u, dst, layer == 1)
+                if held is not None:
+                    net_layer_out(held[0], bias[layer + 1], held[1], held[2], dst, layer == 1)
+                held = (out, b, u)
+        net_layer_out(held[0], bias[layer + 1], held[1], held[2], dst, layer == 1)
     for u in range(4):
         out = jnp.dot(w_last[...], hc[u], preferred_element_type=f32)
         before = taps_of(out[0:16, :])[0]
@@ -548,9 +552,12 @@
         for place in places:
             right(ya, mat_r, yb, bf16, place)
 
-    def leave(g, place):
-        right(yb, mat_l, ff, f32, place)
-        stage3(ff, pr, g, place)
+    def leave(g, places, at):
+        if at == 0:
+            right(yb, mat_l, ff, f32, places[0])
+        if at < 3:
+            right(yb, mat_l, ff, f32, places[at + 1])
+        stage3(ff, pr, g, places[at])
 
     def before_second(k):
         if k == 0:
@@ -571,8 +578,9 @@
         enter(k, 3)
         middle(row_l, row_r, am, ya, yb, ff, functools.partial(before_second, k))
         order = (0, 1) if k == 0 else (1, 0)
+        places = [2 * o + 1 for o in order] + [2 * o for o in order]
         for o in order:
-            leave(g_send.at[k, o], 2 * o + 1)
+            leave(g_send.at[k, o], places, places.index(2 * o + 1))
             rc(g_send.at[k, o], g_recv.at[k, o], gs_sem.at[k, o], gr_sem.at[k, o],
                dev_sib).start()
 
@@ -581,7 +589,7 @@
 
         if k == 0:
             for o in order:
-                leave(g_own.at[o], 2 * o)
+                leave(g_own.at[o], places, places.index(2 * o))
                 arrived(g_recv.at[0, o], gr_sem.at[0, o])
                 for d, (yy, dev) in ((2, around[2]), (0, around[0]), (1, around[1])):
                     sa[d, o] = comb(yy, o).astype(bf16)
@@ -609,7 +617,7 @@
                     left_dev(sa.at[d, o], sa_sem.at[d, o])
         else:
             for o in order:
-                leave(g_own.at[o], 2 * o)
+                leave(g_own.at[o], places, places.index(2 * o))
                 arrived(g_recv.at[1, o], gr_sem.at[1, o])
                 if o == 1:
                     sb[1, 3] = (comb(y, 1) + total[1]).astype(bf16)

time: 72.7 us -> 72.2 us (level)
  no operation moved by 1% of the time
where the time goes in v3:
time: 72.2 us; the launch traced here: 72 us
  Pallas kernels  71.4 us (99%)
    pallas_call x1, Pallas kernels, sweeps(): pl.pallas_call(main_kernel, out_shape=jax.ShapeDtypeStruct((192, N), f32)...  69.6 us
    pallas_call x1, Pallas kernels, split(): pl.pallas_call(split_kernel, out_shape=(jax.ShapeDtypeStruct((128, N), f3...  1.76 us

profile of v3, /device:TPU:0, one launch (start us, length us, event | category | flops | bytes accessed | tf_op | source)
XLA Modules:
  0.0 72.0 jit_solution(10141723538467341397)
XLA Ops:
  0.6 69.6 %shard_map.122.both = f32[192,512]{1,0:T(8,128)} custom-call(f32[2,2,32,512]{3,2,1,0:T(8,128)} %obj.1, f32[2,512,512]{2,1,0:T(8,128)} %probe_hbm.1, f32[2,1,512,512]{3,2,1,0:T(8,128)} %amps_hbm.1, s32[2,1,2]{2,1,0:T(1,128)} %off.1, bf16[4,2,4,256,256]{4,3,2,1,0:T(8,128)(2,1)} %constant.2.clone.mats_hbm, s32[16]{0:T(128)} %slot_angle.1, ...), custom_call_target="tpu_custom_call" | custom-call | flops 12000000000 | bytes 8000000 | tf_op jit(solution)/shard_map/pallas_call | solution.py:760
  70.3 1.8 %shard_map.123 = (f32[128,512]{1,0:T(8,128)}, f32[64,512]{1,0:T(8,128)}) custom-call(f32[192,512]{1,0:T(8,128)} %shard_map.122.both), custom_call_target="tpu_custom_call" | custom-call | tf_op jit(solution)/shard_map/pallas_call | solution.py:678
